TPU v7x, 32 devices: a whole 2x2x4 slice. The times are simulated.
32 devices in a mesh: src: 2 (over y), width: 16 (over z, x, core).
Axes of the slice: x: 2, y: 2, z: 4, core: 2. Of those that a mesh axis runs over, the one named last changes fastest.
Arguments:
- resid: bfloat16 [2, 512, 8192], P('src', None, 'width'), may hold values from -6 to 6
- enc_w: bfloat16 [2, 8192, 6144], P('src', 'width'), may hold values from -0.0625 to 0.0625
- enc_b: float32 [2, 6144], P('src'), may hold values from -3 to 3
- dec_w: bfloat16 [2, 6144, 8192], P('src', None, 'width'), may hold values from -0.078125 to 0.078125
- target: bfloat16 [512, 8192], P(None, 'width'), may hold values from -36 to 36
- norm_gain: float32 [8192], P('width'), may hold values from 0.5 to 1.5
- wq: bfloat16 [8192, 4096], P(None, 'width'), may hold values from -0.0625 to 0.0625
- wk: bfloat16 [8192, 512], P('width'), may hold values from -0.0625 to 0.0625
- wv: bfloat16 [8192, 512], P('width'), may hold values from -0.0625 to 0.0625
- prompt_ids: int32 [512], replicated, may hold values from 0 to 3, never falling along the last dimension, each value on 1 to 256 neighbouring positions
Outputs:
- mlp_out: bfloat16 [512, 8192], P('src', 'width')
- context: bfloat16 [512, 4096], P('src', 'width')
Inputs may be any that keep to these rules, and one draw needn't show every extreme that they name: `prompt_ids`: rows of one prompt are contiguous and numbered in increasing order; the longest prompt has 256 rows.
All inputs are finite; a program needn't handle non-finite values.
Results may differ from a plain program's by a relative error of at most 0.008.
Values may be sent and summed in bfloat16 or wider, within the bound.
A program may use at most 128 MiB of HBM per device.

v0:
```python
import math

import jax
import jax.numpy as jnp
from jax import lax
from jax.sharding import PartitionSpec as P

HD = 128
GROUP = 8


def on_device(resid, enc_w, enc_b, dec_w, target, norm_gain, wq, wk, wv, prompt_ids):
    n_width = lax.axis_size("width")
    n_src = lax.axis_size("src")
    width_pos = lax.axis_index("width")
    rows_all = resid.shape[1]
    width_local = resid.shape[2]
    width_all = width_local * n_width
    feat_share = enc_w.shape[2] // n_width
    mlp = jnp.zeros((rows_all, width_local), jnp.float32)
    local_rows = resid[0]
    w_enc = enc_w[0]
    w_dec = dec_w[0]
    bias = enc_b[0]

    def encode_term(start, count, w_enc=w_enc, local_rows=local_rows):
        return lax.dot_general(
            w_enc, local_rows, (((0,), (1,)), ((), ())), preferred_element_type=jnp.float32
        )

    pre_share = lax.psum_scatter(
        encode_term(jnp.int32(0), feat_share * lax.axis_size("width")),
        "width",
        scatter_dimension=0,
        tiled=True,
    )
    my_bias = lax.dynamic_slice_in_dim(bias, width_pos * feat_share, feat_share, 0)
    feats_t = jnp.maximum(pre_share + my_bias[:, None], 0.0).astype(jnp.bfloat16)

    def decode_piece(total, piece, start, w_dec=w_dec):
        return lax.dot_general(
            piece, w_dec, (((0,), (0,)), ((), ())), preferred_element_type=jnp.float32
        )

    mlp = decode_piece(mlp, lax.all_gather(feats_t, "width", axis=0, tiled=True), jnp.int32(0))
    query_rows = rows_all // n_src
    row_start = lax.axis_index("src") * query_rows
    summed = lax.psum(mlp, "src")
    stream = target.astype(jnp.float32) + summed
    power = lax.psum(jnp.sum(stream * stream, axis=1), "width") / width_all
    normed = (stream * lax.rsqrt(power + 1e-05)[:, None] * norm_gain[None, :]).astype(jnp.bfloat16)
    full = lax.all_gather(normed, "width", axis=1, tiled=True)
    mlp_mine = lax.dynamic_slice_in_dim(summed, row_start, query_rows, 0)
    mlp_out = mlp_mine.astype(jnp.bfloat16)
    mine = lax.dynamic_slice_in_dim(full, row_start, query_rows, 0)
    query = jnp.dot(mine, wq, preferred_element_type=jnp.float32).astype(jnp.bfloat16)
    full_local = lax.dynamic_slice_in_dim(full, width_pos * width_local, width_local, 1)
    key_part = jnp.dot(full_local, wk, preferred_element_type=jnp.float32)
    value_part = jnp.dot(full_local, wv, preferred_element_type=jnp.float32)
    key_total, value_total = lax.psum((key_part, value_part), "width")
    keys_all = key_total.astype(jnp.bfloat16)
    values_all = value_total.astype(jnp.bfloat16)
    heads_here = wq.shape[1] // HD
    kv_index = width_pos * heads_here // GROUP
    key_head = lax.dynamic_slice_in_dim(keys_all, kv_index * HD, HD, 1)
    value_head = lax.dynamic_slice_in_dim(values_all, kv_index * HD, HD, 1)
    query3 = query.reshape(query_rows, heads_here, HD)
    scores = jnp.einsum(
        "qhd,sd->hqs", query3, key_head, preferred_element_type=jnp.float32
    ) / math.sqrt(HD)
    query_index = row_start + jnp.arange(query_rows, dtype=jnp.int32)
    key_index = jnp.arange(rows_all, dtype=jnp.int32)
    query_prompt = lax.dynamic_slice_in_dim(prompt_ids, row_start, query_rows, 0)
    allowed = (query_prompt[:, None] == prompt_ids[None, :]) & (
        key_index[None, :] <= query_index[:, None]
    )
    scores = jnp.where(allowed[None], scores, -1e30)
    peak = jnp.max(scores, axis=-1, keepdims=True)
    weights = jnp.exp(scores - peak)
    probs = (weights / jnp.sum(weights, axis=-1, keepdims=True)).astype(jnp.bfloat16)
    context = jnp.einsum("hqs,sd->qhd", probs, value_head, preferred_element_type=jnp.float32)
    return (mlp_out, context.reshape(query_rows, heads_here * HD).astype(jnp.bfloat16))


def solution(mesh):
    in_specs = (
        P("src", None, "width"),
        P("src", "width", None),
        P("src", None),
        P("src", None, "width"),
        P(None, "width"),
        P("width"),
        P(None, "width"),
        P("width", None),
        P("width", None),
        P(),
    )
    out_specs = (P("src", "width"), P("src", "width"))
    return jax.shard_map(
        on_device, mesh=mesh, in_specs=in_specs, out_specs=out_specs, check_vma=False
    )
```

profile of v0, /device:TPU:0, one launch (start us, length us, event | category | flops | bytes accessed | tf_op | source)
XLA Modules:
  0.0 468.9 jit_solution(6628273000042261011)
XLA Ops:
  7.2 0.0 copy-start
  7.2 0.0 reduce-scatter.2.cloned.1.call-start
  7.2 1.0 copy-done
  8.2 9.4 %fusion.3 = f32[6144,512]{1,0:T(8,128)} fusion(bf16[1,512,6144]{2,1,0:T(8,128)(2,1)} %param.11, bf16[1,512,512]{2,1,0:T(8,128)(2,1)S(1)} %copy-done), kind=kOutput, calls=%fused_computation.3 | convolution fusion | flops 3221225472 | bytes 19398656 | tf_op jit(solution)/shard_map/dot_general | solution.py:27
  17.6 0.0 reduce-scatter.2.cloned.1.call-update
  17.6 0.0 all-gather.3.cloned.1.call-start
  17.6 0.7 dynamic-slice_reduce_fusion
  18.3 136.7 %reduce-scatter.2.cloned.1.call-done = f32[384,512]{1,0:T(8,128)} async-done(((f32[6144,512]{1,0:T(8,128)}), f32[384,512]{1,0:T(8,128)}) %reduce-scatter.2.cloned.1.call-update) | async-done | bytes 786448 | tf_op jit(solution)/shard_map/reduce_scatter | solution.py:31
  155.1 2.0 maximum_convert_fusion
  157.1 0.0 all-gather.3.cloned.1.call-update
  157.1 0.0 copy-start.1
  157.1 0.0 copy-start.5
  157.1 0.0 copy-start.4
  157.2 0.0 all-reduce.4.cloned.1.call-start
  157.2 61.1 %all-gather.3.cloned.1.call-done = bf16[6144,512]{1,0:T(8,128)(2,1)} async-done(((bf16[384,512]{1,0:T(8,128)(2,1)}), bf16[6144,512]{1,0:T(8,128)(2,1)}) %all-gather.3.cloned.1.call-update) | async-done | bytes 6291472 | tf_op jit(solution)/shard_map/all_gather | solution.py:45
  218.4 9.0 %fusion.1 = f32[512,512]{1,0:T(8,128)} fusion(bf16[6144,512]{1,0:T(8,128)(2,1)} %all-gather.3.cloned.1.call-done, bf16[1,6144,512]{2,1,0:T(8,128)(2,1)} %param.13), kind=kOutput, calls=%fused_computation.1 | convolution fusion | flops 3221225472 | bytes 13631488 | tf_op jit(solution)/shard_map/dot_general | solution.py:41
  227.4 0.0 copy-start.2
  227.4 0.0 copy-start.3
  227.4 0.0 all-reduce.4.cloned.1.call-update
  227.4 0.0 all-gather.5.cloned.1.call-start
  227.5 38.8 %all-reduce.4.cloned.1.call-done = f32[512,512]{1,0:T(8,128)} async-done(((f32[512,512]{1,0:T(8,128)}), f32[512,512]{1,0:T(8,128)}) %all-reduce.4.cloned.1.call-update) | async-done | bytes 1048592 | tf_op jit(solution)/shard_map/psum | solution.py:48
  266.2 0.0 copy-done.1
  266.2 1.4 multiply_reduce_fusion
  267.7 33.2 %psum.29 = f32[512]{0:T(512)S(1)} all-reduce(f32[512]{0:T(512)S(1)} %multiply_reduce_fusion), channel_id=1, replica_groups=mesh['src'=2,'width'=16] {'width'}, use_global_device_ids=true, to_apply=%region_3.0 | all-reduce | flops 512 | bytes 4096 | tf_op jit(solution)/shard_map/psum | solution.py:50
  300.8 0.0 copy-done.5
  300.8 2.2 multiply_convert_fusion
  303.0 0.0 all-gather.5.cloned.1.call-update
  303.1 0.0 copy-done.4
  303.1 0.1 dynamic_slice.25
  303.2 0.1 fusion.15
  303.3 1.8 dynamic-slice_convert_fusion
  305.1 72.5 %all-gather.5.cloned.1.call-done = bf16[512,8192]{1,0:T(8,128)(2,1)} async-done(((bf16[512,512]{1,0:T(8,128)(2,1)}), bf16[512,8192]{1,0:T(8,128)(2,1)}) %all-gather.5.cloned.1.call-update) | async-done | bytes 8388624 | tf_op jit(solution)/shard_map/all_gather | solution.py:52
  377.6 0.0 copy-done.2
  377.6 1.5 fusion.16
  379.1 0.0 copy-done.3
  379.1 1.5 fusion.18
  380.7 73.7 %all-reduce.5 = (bf16[512,512]{1,0:T(8,128)(2,1)S(1)}, bf16[512,512]{0,1:T(8,128)(2,1)}) all-reduce(f32[512,512]{1,0:T(8,128)S(1)} %fusion.16, f32[512,512]{0,1:T(8,128)S(1)} %fusion.18), channel_id=1, replica_groups=mesh['src'=2,'width'=16] {'width'}, use_global_device_ids=true, to_apply=%region_5.0 | all-reduce | flops 524288 | bytes 3145728 | tf_op jit(solution)/shard_map/psum | solution.py:60
  454.3 5.2 %fusion.11 = bf16[256,256]{0,1:T(8,128)(2,1)S(1)} fusion(bf16[8192,256]{1,0:T(8,128)(2,1)} %param.16, bf16[512,8192]{1,0:T(8,128)(2,1)} %all-gather.5.cloned.1.call-done, s32[]{:T(128)S(6)} %select_n.25), kind=kOutput, calls=%fused_computation.13 | convolution fusion | flops 1073807360 | bytes 8519684 | tf_op jit(solution)/shard_map/dot_general | solution.py:56
  459.5 0.5 fusion.36
  460.0 0.3 fusion.10
  460.3 1.3 convolution_convert_fusion
  461.6 0.8 copy.14
  (2 shorter events, 0.0 us)
Async XLA Ops:
  7.2 1.0 copy-start
  7.2 147.9 %reduce-scatter.2.cloned.1.call-start = ((), (), s32[]{:S(2)}) async-start(), calls=%async_computation.1 | async-start | bytes 13369344 | tf_op jit(solution)/shard_map/reduce_scatter | solution.py:31
  17.6 200.8 %all-gather.3.cloned.1.call-start = ((), (), s32[]{:S(2)}) async-start(), calls=%async_computation.2 | async-start | bytes 6684672 | tf_op jit(solution)/shard_map/all_gather | solution.py:45
  157.1 109.1 %copy-start.1 = (bf16[512,512]{1,0:T(8,128)(2,1)S(1)}, bf16[512,512]{1,0:T(8,128)(2,1)}, u32[]{:S(2)}) copy-start(bf16[512,512]{1,0:T(8,128)(2,1)} %param.14) | copy-start | bytes 1572868
  157.1 143.7 %copy-start.5 = (f32[512]{0:T(512)S(1)}, f32[512]{0:T(512)}, u32[]{:S(2)}) copy-start(f32[512]{0:T(512)} %param.15) | copy-start | bytes 6148
  157.1 145.9 %copy-start.4 = (s32[512]{0:T(512)S(1)}, s32[512]{0:T(512)}, u32[]{:S(2)}) copy-start(s32[512]{0:T(512)} %param.19) | copy-start | bytes 6148
  157.2 109.1 %all-reduce.4.cloned.1.call-start = ((), (), s32[]{:S(2)}) async-start(), calls=%async_computation.3 | async-start | bytes 2097152 | tf_op jit(solution)/shard_map/psum | solution.py:48
  227.4 150.2 %copy-start.2 = (bf16[512,512]{1,0:T(8,128)(2,1)S(1)}, bf16[512,512]{1,0:T(8,128)(2,1)}, u32[]{:S(2)}) copy-start(bf16[512,512]{1,0:T(8,128)(2,1)} %param.17) | copy-start | bytes 1572868
  227.4 151.7 %copy-start.3 = (bf16[512,512]{1,0:T(8,128)(2,1)S(1)}, bf16[512,512]{1,0:T(8,128)(2,1)}, u32[]{:S(2)}) copy-start(bf16[512,512]{1,0:T(8,128)(2,1)} %param.18) | copy-start | bytes 1572868
  227.4 150.2 %all-gather.5.cloned.1.call-start = ((), (), s32[]{:S(2)}) async-start(), calls=%async_computation.4 | async-start | bytes 8912896 | tf_op jit(solution)/shard_map/all_gather | solution.py:52
Sparse Core Ops, SparseCore 0:
  17.7 137.3 reduce-scatter.1
  157.3 60.9 all-gather.2
  227.5 38.6 all-reduce.3
  303.2 74.3 all-gather.4
where the time goes:
time: 469 us
  waiting for transfers between devices  309 us (66%)
  blocking collectives  107 us (23%)
  matrix products  28.7 us (6%)
  between operations  13.9 us (3%)
  other arithmetic  5.82 us (1%)
    reduce_scatter x1, waiting for transfers between devices, on_device(): lax.psum_scatter(encode_term(jnp.int32(0), feat_share * lax.axis_size('wi...  137 us
    psum x1, blocking collectives, on_device(): key_total, value_total = lax.psum((key_part, value_part), 'width')  73.7 us
    all_gather x1, waiting for transfers between devices, on_device(): full = lax.all_gather(normed, 'width', axis=1, tiled=True)  72.5 us
    all_gather x1, waiting for transfers between devices, on_device(): lax.all_gather(feats_t, 'width', axis=0, tiled=True)  61.1 us
    psum x1, waiting for transfers between devices, on_device(): summed = lax.psum(mlp, 'src')  38.8 us
    psum x1, blocking collectives, on_device(): power = lax.psum(jnp.sum(stream * stream, axis=1), 'width') / width_all  33.2 us
  transfers between devices with their start and end apart: 4, of which 4 were waited for; matrix products, arithmetic and copies ran while one was open for 1% of the time, Pallas kernels for 0%

commit v1 on v0

v1 whole, which is shorter than its diff:
```python
import functools
import math

import jax
import jax.numpy as jnp
from jax import lax
from jax.experimental import pallas as pl
from jax.experimental.pallas import tpu as pltpu
from jax.sharding import PartitionSpec as P

HD = 128
GROUP = 8
NC = 2
NZ = 4
T = 4
BF = jnp.bfloat16
F32 = jnp.float32


def dot(a, b):
    return jnp.dot(a, b, preferred_element_type=F32)


def kernel(
    n, n_src,
    resid, enc_w, enc_b, dec_w, target, gain, wq, wk, wv, ids_row, ids_col,
    mlp_out, context,
    rs_v, e_v, d_v, t_v, q_v, k_v, v_v,
    part, c_buf, x_buf, z_buf, feats, acc, y_send, y_buf,
    full, pw, r_col, kvp, kvr, kv, qacc,
    load_sem, c_sem, x_sem, z_sem, gz_sem, gx_sem, gc_sem, y_sem, f_sem, p_sem, kr_sem, kg_sem,
):
    nx = n // (NC * NZ)
    rows = resid.shape[1]
    share = resid.shape[2]
    fc = enc_w.shape[2] // T
    R = rows // n_src
    H, X, Z = rows // NC, rows // (NC * nx), rows // n
    w = lax.axis_index("width")
    s = lax.axis_index("src")
    c = lax.rem(w, NC)
    x = lax.rem(w // NC, nx)
    z = w // (NC * nx)
    members = 4
    g, m = w // members, lax.rem(w, members)
    n_kv = n // members
    RQ = R // members

    def wid(zz, xx, cc):
        return (zz * nx + xx) * NC + cc

    def plus(v, k, size):
        return lax.rem(v + k, size)

    def minus(v, k, size):
        return lax.rem(v + size - k, size)

    def ds(start, size):
        return pl.ds(pl.multiple_of(start, size), size)

    loads = []

    def load(i, src, dst):
        cp = pltpu.make_async_copy(src, dst, load_sem.at[i])
        cp.start()
        loads.append(cp)
        return cp

    ld_resid = load(0, resid.at[0], rs_v)
    ld_e = [load(1 + t, enc_w.at[0, :, pl.ds(t * fc, fc)], e_v.at[t]) for t in range(T)]
    ld_d = load(T + 1, dec_w.at[0], d_v)
    ld_t = load(T + 2, target.at[ds(s * R, R)], t_v)
    ld_k = load(T + 3, wk, k_v)
    ld_v = load(T + 4, wv, v_v)
    ld_q = load(T + 5, wq, q_v)

    barrier = pltpu.get_barrier_semaphore()
    for k in range(1, n):
        pl.semaphore_signal(barrier, inc=1, device_id={"src": s, "width": plus(w, k, n)})
    for ks in range(1, n_src):
        for mm in range(members):
            pl.semaphore_signal(
                barrier, inc=1,
                device_id={"src": plus(s, ks, n_src), "width": g * members + mm},
            )

    sends = []

    def rdma(src, dst, sems, i, dev):
        return pltpu.make_async_remote_copy(
            src_ref=src, dst_ref=dst, send_sem=sems.at[(0,) + i], recv_sem=sems.at[(1,) + i],
            device_id=dev, device_id_type=pl.DeviceIdType.MESH,
        )

    def send(src, dst, sems, i, ww=None, ss=None):
        cp = rdma(src, dst, sems, i, {"src": s if ss is None else ss, "width": w if ww is None else ww})
        cp.start()
        sends.append(cp)

    def arrive(dst, sems, i):
        rdma(dst, dst, sems, i, {"src": s, "width": plus(w, 1, n)}).wait_recv()

    sibling = wid(z, x, 1 - c)
    c0 = c * H
    x0 = c0 + x * X
    z0 = x0 + z * Z

    def encode(t):
        ld_e[t].wait()
        step = 512 if fc % 512 == 0 else fc

        @pl.loop(0, fc // step)
        def _(j):
            cols = ds(j * step, step)
            part[t, :, cols] = dot(rs_v[...], e_v[t, :, cols]).astype(BF)

    def rs_c(t):
        send(part.at[t, ds((1 - c) * H, H)], c_buf.at[t], c_sem, (t,), sibling)

    def rs_x(t):
        arrive(c_buf.at[t], c_sem, (t,))

        def add(xx):
            @pl.loop(0, X // Z)
            def _(j):
                a = ds(c0 + xx * X + j * Z, Z)
                b = ds(xx * X + j * Z, Z)
                part[t, a] = (part[t, a].astype(F32) + c_buf[t, b].astype(F32)).astype(BF)

        for k in range(1, nx):
            xx = plus(x, k, nx)
            add(xx)
            send(part.at[t, ds(c0 + xx * X, X)], x_buf.at[t, k - 1], x_sem, (t, k - 1), wid(z, xx, c))
        add(x)

    def rs_z(t):
        for k in range(1, nx):
            arrive(x_buf.at[t, k - 1], x_sem, (t, k - 1))

        def add(zz):
            a = ds(x0 + zz * Z, Z)
            b = ds(zz * Z, Z)
            total = part[t, a].astype(F32)
            for k in range(1, nx):
                total += x_buf[t, k - 1, b].astype(F32)
            part[t, a] = total.astype(BF)

        for k in (2, 1, 3):
            zz = plus(z, k, NZ)
            add(zz)
            send(part.at[t, ds(x0 + zz * Z, Z)], z_buf.at[t, k - 1], z_sem, (t, k - 1), wid(zz, x, c))
        add(z)

    def ag_z(t):
        for k in range(1, NZ):
            arrive(z_buf.at[t, k - 1], z_sem, (t, k - 1))
        own = ds(z0, Z)
        total = part[t, own].astype(F32) + enc_b[:, pl.ds(t * fc, fc)]
        for k in range(1, NZ):
            total += z_buf[t, k - 1].astype(F32)
        feats[t, own] = jnp.maximum(total, 0.0).astype(BF)
        for k in (2, 1, 3):
            send(feats.at[t, own], feats.at[t, own], gz_sem, (t, k - 1), wid(plus(z, k, NZ), x, c))

    def ag_x(t):
        for k in range(1, NZ):
            arrive(feats.at[t, ds(x0 + minus(z, k, NZ) * Z, Z)], gz_sem, (t, k - 1))
        own = ds(x0, X)
        for k in range(1, nx):
            send(feats.at[t, own], feats.at[t, own], gx_sem, (t, k - 1), wid(z, plus(x, k, nx), c))

    def ag_c(t):
        for k in range(1, nx):
            arrive(feats.at[t, ds(c0 + minus(x, k, nx) * X, X)], gx_sem, (t, k - 1))
        own = ds(c0, H)
        send(feats.at[t, own], feats.at[t, own], gc_sem, (t,), sibling)

    def decode_rows(t, start):
        r = ds(start, R)
        p = dot(feats[t, r], d_v[pl.ds(t * fc, fc), :])
        if t == 0:
            acc[r, :] = p
        else:
            acc[r, :] += p

    def decode(t):
        arrive(feats.at[t, ds((1 - c) * H, H)], gc_sem, (t,))
        if t == 0:
            ld_d.wait()
        for k in range(1, n_src):
            ss = plus(s, k, n_src)
            decode_rows(t, ss * R)
            if t == T - 1:
                y_send[k - 1] = acc[ds(ss * R, R), :].astype(BF)
                send(y_send.at[k - 1], y_buf.at[k - 1], y_sem, (k - 1,), None, ss)
        decode_rows(t, s * R)

    ld_resid.wait()
    encode(0)
    pl.semaphore_wait(barrier, n - 1 + (n_src - 1) * members)
    rs_c(0)
    for t in range(1, T):
        encode(t)
        rs_c(t)
    stages = (rs_x, rs_z, ag_z, ag_x, ag_c, decode)
    for tick in range(T + len(stages) - 1):
        for i in reversed(range(len(stages))):
            if 0 <= tick - i < T:
                stages[i](tick - i)

    for k in range(1, n_src):
        arrive(y_buf.at[k - 1], y_sem, (k - 1,))
    mlp = acc[ds(s * R, R), :]
    for k in range(1, n_src):
        mlp += y_buf[k - 1].astype(F32)
    mlp_out[...] = mlp.astype(BF)
    ld_t.wait()
    stream = t_v[...].astype(F32) + mlp

    def slot(cc, xx, zz):
        return (cc * nx + xx) * NZ + zz

    me = slot(c, x, z)
    full[me] = (stream * gain[...]).astype(BF)

    def forward(cc_done, kx, kz, at):
        if kx == 0:
            for k in range(1, nx):
                send(full.at[at], full.at[at], f_sem, (0, k, kz), wid(z, plus(x, k, nx), c))
        send(full.at[at], full.at[at], f_sem, (1, kx, kz), sibling)

    for k in (2, 1, 3):
        send(full.at[me], full.at[me], f_sem, (0, 0, k), wid(plus(z, k, NZ), x, c))
    forward(0, 0, 0, me)

    sq = lax.dot_general(
        jnp.ones((8, share), F32), stream * stream, (((1,), (1,)), ((), ())),
        precision=lax.Precision.HIGHEST, preferred_element_type=F32,
    )
    pw[0] = sq
    for k in range(1, n):
        send(pw.at[0], pw.at[k], p_sem, (k - 1,), plus(w, k, n))

    ld_k.wait()
    ld_v.wait()
    kp = dot(full[me], k_v[...]).astype(BF)
    vp = dot(full[me], v_v[...]).astype(BF)
    for h in range(n_kv):
        kvp[h, :, 0:HD] = kp[:, h * HD:(h + 1) * HD]
        kvp[h, :, HD:2 * HD] = vp[:, h * HD:(h + 1) * HD]
    for k in range(1, n):
        ww = plus(w, k, n)
        send(kvp.at[ww // members, ds(lax.rem(ww, members) * RQ, RQ)], kvr.at[k - 1], kr_sem, (k - 1,), ww)

    def add_query(at, origin):
        qacc[...] += dot(full[at], q_v[ds(origin * share, share), :])

    ld_q.wait()
    qacc[...] = dot(full[me], q_v[ds(w * share, share), :])
    for kz in (1, 2, 3):
        zz = minus(z, kz, NZ)
        at = slot(c, x, zz)
        arrive(full.at[at], f_sem, (0, 0, kz))
        forward(0, 0, kz, at)
        add_query(at, wid(zz, x, c))

    total = pw[0]
    for k in range(1, n):
        arrive(pw.at[k], p_sem, (k - 1,))
    for k in range(1, n):
        total += pw[k]
    r_col[...] = jnp.transpose(lax.rsqrt(total / (share * n) + 1e-05))
    for k in range(1, n):
        arrive(kvr.at[k - 1], kr_sem, (k - 1,))
    mine = kvp[g, ds(m * RQ, RQ)].astype(F32)
    for k in range(1, n):
        mine += kvr[k - 1].astype(F32)
    out_rows = ds(s * R + m * RQ, RQ)
    kv[out_rows, :] = (mine * r_col[ds(m * RQ, RQ), 0:1]).astype(BF)
    for ks in range(n_src):
        for km in range(members):
            if ks or km:
                send(
                    kv.at[out_rows], kv.at[out_rows], kg_sem, (ks, km),
                    g * members + plus(m, km, members), plus(s, ks, n_src),
                )

    for kx in range(1, nx):
        xx = minus(x, kx, nx)
        for kz in range(NZ):
            zz = minus(z, kz, NZ)
            at = slot(c, xx, zz)
            arrive(full.at[at], f_sem, (0, kx, kz))
            forward(0, kx, kz, at)
            add_query(at, wid(zz, xx, c))
    for kx in range(nx):
        xx = minus(x, kx, nx)
        for kz in range(NZ):
            zz = minus(z, kz, NZ)
            at = slot(1 - c, xx, zz)
            arrive(full.at[at], f_sem, (1, kx, kz))
            add_query(at, wid(zz, xx, 1 - c))

    for ks in range(n_src):
        for km in range(members):
            if ks or km:
                at = minus(s, ks, n_src) * R + minus(m, km, members) * RQ
                arrive(kv.at[ds(at, RQ)], kg_sem, (ks, km))

    query = (qacc[...] * r_col[:, 0:1]).astype(BF)
    qi = s * R + lax.broadcasted_iota(jnp.int32, (R, rows), 0)
    ki = lax.broadcasted_iota(jnp.int32, (R, rows), 1)
    allowed = (ids_col[...] == ids_row[...]) & (ki <= qi)
    for h in range(query.shape[1] // HD):
        scores = lax.dot_general(
            query[:, h * HD:(h + 1) * HD], kv[:, 0:HD], (((1,), (1,)), ((), ())),
            preferred_element_type=F32,
        ) * (1.0 / math.sqrt(HD))
        scores = jnp.where(allowed, scores, -1e30)
        peak = jnp.max(scores, axis=-1, keepdims=True)
        weights = jnp.exp(scores - peak)
        probs = (weights / jnp.sum(weights, axis=-1, keepdims=True)).astype(BF)
        context[:, h * HD:(h + 1) * HD] = dot(probs, kv[:, HD:2 * HD]).astype(BF)

    for cp in sends:
        cp.wait_send()


def on_device(resid, enc_w, enc_b, dec_w, target, norm_gain, wq, wk, wv, prompt_ids):
    n = lax.axis_size("width")
    n_src = lax.axis_size("src")
    rows, share = resid.shape[1:]
    fc = enc_w.shape[2] // T
    R = rows // n_src
    nx = n // (NC * NZ)
    H, X, Z = rows // NC, rows // (NC * nx), rows // n
    members = 4
    n_kv = n // members
    RQ = R // members
    ids_col = lax.dynamic_slice_in_dim(prompt_ids, lax.axis_index("src") * R, R, 0)[:, None]
    any_ = pl.BlockSpec(memory_space=pl.ANY)
    vm = pl.BlockSpec(memory_space=pltpu.VMEM)
    dma = pltpu.SemaphoreType.DMA
    nx1 = max(nx - 1, 1)
    ns1 = max(n_src - 1, 1)
    return pl.pallas_call(
        functools.partial(kernel, n, n_src),
        out_shape=(
            jax.ShapeDtypeStruct((R, share), BF),
            jax.ShapeDtypeStruct((R, wq.shape[1]), BF),
        ),
        in_specs=[any_, any_, vm, any_, any_, vm, any_, any_, any_, vm, vm],
        out_specs=(vm, vm),
        scratch_shapes=[
            pltpu.VMEM((rows, share), BF),
            pltpu.VMEM((T, share, fc), BF),
            pltpu.VMEM((T * fc, share), BF),
            pltpu.VMEM((R, share), BF),
            pltpu.VMEM(wq.shape, BF),
            pltpu.VMEM(wk.shape, BF),
            pltpu.VMEM(wv.shape, BF),
            pltpu.VMEM((T, rows, fc), BF),
            pltpu.VMEM((T, H, fc), BF),
            pltpu.VMEM((T, nx1, X, fc), BF),
            pltpu.VMEM((T, NZ - 1, Z, fc), BF),
            pltpu.VMEM((T, rows, fc), BF),
            pltpu.VMEM((rows, share), F32),
            pltpu.VMEM((ns1, R, share), BF),
            pltpu.VMEM((ns1, R, share), BF),
            pltpu.VMEM((n, R, share), BF),
            pltpu.VMEM((n, 8, R), F32),
            pltpu.VMEM((R, 8), F32),
            pltpu.VMEM((n_kv, R, 2 * HD), BF),
            pltpu.VMEM((n - 1, RQ, 2 * HD), BF),
            pltpu.VMEM((rows, 2 * HD), BF),
            pltpu.VMEM((R, wq.shape[1]), F32),
            dma((T + 6,)),
            dma((2, T)),
            dma((2, T, nx1)),
            dma((2, T, NZ - 1)),
            dma((2, T, NZ - 1)),
            dma((2, T, nx1)),
            dma((2, T)),
            dma((2, ns1)),
            dma((2, 2, nx, NZ)),
            dma((2, n - 1)),
            dma((2, n - 1)),
            dma((2, n_src, members)),
        ],
        compiler_params=pltpu.CompilerParams(
            collective_id=0, has_side_effects=True, vmem_limit_bytes=60 * 1024 * 1024
        ),
    )(resid, enc_w, enc_b, dec_w, target, norm_gain[None, :], wq, wk, wv, prompt_ids[None, :], ids_col)


def solution(mesh):
    in_specs = (
        P("src", None, "width"),
        P("src", "width", None),
        P("src", None),
        P("src", None, "width"),
        P(None, "width"),
        P("width"),
        P(None, "width"),
        P("width", None),
        P("width", None),
        P(),
    )
    out_specs = (P("src", "width"), P("src", "width"))
    return jax.shard_map(
        on_device, mesh=mesh, in_specs=in_specs, out_specs=out_specs, check_vma=False
    )
```

time: 469 us -> 174 us (0.37)
  the two profiles are of different devices: /device:TPU:0 before, /device:TPU:19 now
where the time goes in v1:
time: 174 us
  Pallas kernels  169 us (97%)
  local copies, waits for them, and re-layouts  4.8 us (3%)
    pallas_call x1, Pallas kernels, on_device(): pl.pallas_call(functools.partial(kernel, n, n_src), out_shape=(jax.ShapeD...  169 us

profile of v1, /device:TPU:19, one launch (start us, length us, event | category | flops | bytes accessed | tf_op | source)
XLA Modules:
  0.0 174.2 jit_solution(1613691097085457047)
XLA Ops:
  0.6 0.8 dynamic_slice.3
  1.4 0.8 copy.12.ids_col
  2.2 168.8 %shard_map.113 = (bf16[256,512]{1,0:T(8,128)(2,1)}, bf16[256,256]{1,0:T(8,128)(2,1)}) custom-call(bf16[1,512,512]{2,1,0:T(8,128)(2,1)} %resid.1, bf16[1,512,6144]{2,1,0:T(8,128)(2,1)} %enc_w.1, f32[1,6144]{1,0:T(1,128)} %enc_b.1, bf16[1,6144,512]{2,1,0:T(8,128)(2,1)} %dec_w.1, bf16[512,512]{1,0:T(8,128)(2,1)} %target.1, f32[1,512]{1,0:T(1,128)} %bitcast.5, ...), custom_call_target="tpu_custom_call" | custom-call | tf_op jit(solution)/shard_map/pallas_call | solution.py:346
  171.0 1.7 copy.15
  172.7 1.6 copy.16

commit v2 on v1

--- a/solution.py
+++ b/solution.py
@@ -12,7 +12,7 @@
 GROUP = 8
 NC = 2
 NZ = 4
-T = 4
+T = 6
 BF = jnp.bfloat16
 F32 = jnp.float32
 
@@ -27,8 +27,8 @@
     mlp_out, context,
     rs_v, e_v, d_v, t_v, q_v, k_v, v_v,
     part, c_buf, x_buf, z_buf, feats, acc, y_send, y_buf,
-    full, pw, r_col, kvp, kvr, kv, qacc,
-    load_sem, c_sem, x_sem, z_sem, gz_sem, gx_sem, gc_sem, y_sem, f_sem, p_sem, kr_sem, kg_sem,
+    full, pw, r_col, kvp, kvr, kvs, kvt, kv, qacc,
+    load_sem, c_sem, x_sem, z_sem, gz_sem, gx_sem, gc_sem, y_sem, f_sem, p_sem, kr_sem, kt_sem, kg_sem,
 ):
     nx = n // (NC * NZ)
     rows = resid.shape[1]
@@ -202,9 +202,11 @@
     for t in range(1, T):
         encode(t)
         rs_c(t)
-    stages = (rs_x, rs_z, ag_z, ag_x, ag_c, decode)
+        rs_x(t - 1)
+    rs_x(T - 1)
+    stages = (rs_z, ag_z, ag_x, ag_c, decode)
     for tick in range(T + len(stages) - 1):
-        for i in reversed(range(len(stages))):
+        for i in range(len(stages)):
             if 0 <= tick - i < T:
                 stages[i](tick - i)
 
@@ -245,12 +247,13 @@
     ld_v.wait()
     kp = dot(full[me], k_v[...]).astype(BF)
     vp = dot(full[me], v_v[...]).astype(BF)
-    for h in range(n_kv):
-        kvp[h, :, 0:HD] = kp[:, h * HD:(h + 1) * HD]
-        kvp[h, :, HD:2 * HD] = vp[:, h * HD:(h + 1) * HD]
-    for k in range(1, n):
-        ww = plus(w, k, n)
-        send(kvp.at[ww // members, ds(lax.rem(ww, members) * RQ, RQ)], kvr.at[k - 1], kr_sem, (k - 1,), ww)
+    for mm in range(members):
+        for h in range(n_kv):
+            kvp[mm, h, :, 0:HD] = kp[mm * RQ:(mm + 1) * RQ, h * HD:(h + 1) * HD]
+            kvp[mm, h, :, HD:2 * HD] = vp[mm * RQ:(mm + 1) * RQ, h * HD:(h + 1) * HD]
+    for k in (2, 1, 3):
+        mm = plus(m, k, members)
+        send(kvp.at[mm], kvr.at[k - 1], kr_sem, (k - 1,), g * members + mm)
 
     def add_query(at, origin):
         qacc[...] += dot(full[at], q_v[ds(origin * share, share), :])
@@ -264,17 +267,35 @@
         forward(0, 0, kz, at)
         add_query(at, wid(zz, x, c))
 
+    for k in range(1, members):
+        arrive(kvr.at[k - 1], kr_sem, (k - 1,))
+    group = kvp[m].astype(F32)
+    for k in range(1, members):
+        group += kvr[k - 1].astype(F32)
+    kvs[...] = group.astype(BF)
+    for k in range(1, n_kv):
+        gg = plus(g, k, n_kv)
+        send(kvs.at[gg], kvt.at[k - 1], kt_sem, (k - 1,), gg * members + m)
+
+    for kx in range(1, nx):
+        xx = minus(x, kx, nx)
+        for kz in range(NZ):
+            zz = minus(z, kz, NZ)
+            at = slot(c, xx, zz)
+            arrive(full.at[at], f_sem, (0, kx, kz))
+            forward(0, kx, kz, at)
+            add_query(at, wid(zz, xx, c))
     total = pw[0]
     for k in range(1, n):
         arrive(pw.at[k], p_sem, (k - 1,))
     for k in range(1, n):
         total += pw[k]
     r_col[...] = jnp.transpose(lax.rsqrt(total / (share * n) + 1e-05))
-    for k in range(1, n):
-        arrive(kvr.at[k - 1], kr_sem, (k - 1,))
-    mine = kvp[g, ds(m * RQ, RQ)].astype(F32)
-    for k in range(1, n):
-        mine += kvr[k - 1].astype(F32)
+    for k in range(1, n_kv):
+        arrive(kvt.at[k - 1], kt_sem, (k - 1,))
+    mine = kvs[g].astype(F32)
+    for k in range(1, n_kv):
+        mine += kvt[k - 1].astype(F32)
     out_rows = ds(s * R + m * RQ, RQ)
     kv[out_rows, :] = (mine * r_col[ds(m * RQ, RQ), 0:1]).astype(BF)
     for ks in range(n_src):
@@ -285,14 +306,6 @@
                     g * members + plus(m, km, members), plus(s, ks, n_src),
                 )
 
-    for kx in range(1, nx):
-        xx = minus(x, kx, nx)
-        for kz in range(NZ):
-            zz = minus(z, kz, NZ)
-            at = slot(c, xx, zz)
-            arrive(full.at[at], f_sem, (0, kx, kz))
-            forward(0, kx, kz, at)
-            add_query(at, wid(zz, xx, c))
     for kx in range(nx):
         xx = minus(x, kx, nx)
         for kz in range(NZ):
@@ -370,8 +383,10 @@
             pltpu.VMEM((n, R, share), BF),
             pltpu.VMEM((n, 8, R), F32),
             pltpu.VMEM((R, 8), F32),
-            pltpu.VMEM((n_kv, R, 2 * HD), BF),
-            pltpu.VMEM((n - 1, RQ, 2 * HD), BF),
+            pltpu.VMEM((members, n_kv, RQ, 2 * HD), BF),
+            pltpu.VMEM((members - 1, n_kv, RQ, 2 * HD), BF),
+            pltpu.VMEM((n_kv, RQ, 2 * HD), BF),
+            pltpu.VMEM((n_kv - 1, RQ, 2 * HD), BF),
             pltpu.VMEM((rows, 2 * HD), BF),
             pltpu.VMEM((R, wq.shape[1]), F32),
             dma((T + 6,)),
@@ -384,7 +399,8 @@
             dma((2, ns1)),
             dma((2, 2, nx, NZ)),
             dma((2, n - 1)),
-            dma((2, n - 1)),
+            dma((2, members - 1)),
+            dma((2, n_kv - 1)),
             dma((2, n_src, members)),
         ],
         compiler_params=pltpu.CompilerParams(

time: 174 us -> 161 us (0.925)
  Pallas kernels: 169 us -> 155 us
    pallas_call x1, Pallas kernels: 169 us -> 155 us  [on_device(): pl.pallas_call(functools.partial(kernel, n, n_src), out_shape=(jax.ShapeD...]
where the time goes in v2:
time: 161 us
  Pallas kernels  155 us (96%)
  local copies, waits for them, and re-layouts  4.8 us (3%)
    pallas_call x1, Pallas kernels, on_device(): pl.pallas_call(functools.partial(kernel, n, n_src), out_shape=(jax.ShapeD...  155 us
    unnamed x2, local copies, waits for them, and re-layouts  3.24 us

profile of v2, /device:TPU:19, one launch (start us, length us, event | category | flops | bytes accessed | tf_op | source)
XLA Modules:
  0.0 160.9 jit_solution(10299976155819647199)
XLA Ops:
  0.6 0.8 dynamic_slice.3
  1.4 0.8 copy.12.ids_col
  2.2 155.5 %shard_map.113 = (bf16[256,512]{1,0:T(8,128)(2,1)}, bf16[256,256]{1,0:T(8,128)(2,1)}) custom-call(bf16[1,512,512]{2,1,0:T(8,128)(2,1)} %resid.1, bf16[1,512,6144]{2,1,0:T(8,128)(2,1)} %enc_w.1, f32[1,6144]{1,0:T(1,128)} %enc_b.1, bf16[1,6144,512]{2,1,0:T(8,128)(2,1)} %dec_w.1, bf16[512,512]{1,0:T(8,128)(2,1)} %target.1, f32[1,512]{1,0:T(1,128)} %bitcast.5, ...), custom_call_target="tpu_custom_call" | custom-call | tf_op jit(solution)/shard_map/pallas_call | solution.py:359
  157.7 1.7 %copy.15 = bf16[256,512]{1,0:T(8,128)(2,1)} copy(bf16[256,512]{1,0:T(8,128)(2,1)} %get-tuple-element.4) | data formatting | bytes 524288
  159.3 1.6 copy.16

commit v3 on v2

--- a/solution.py
+++ b/solution.py
@@ -163,15 +163,18 @@
             send(feats.at[t, own], feats.at[t, own], gz_sem, (t, k - 1), wid(plus(z, k, NZ), x, c))
 
     def ag_x(t):
-        for k in range(1, NZ):
-            arrive(feats.at[t, ds(x0 + minus(z, k, NZ) * Z, Z)], gz_sem, (t, k - 1))
-        own = ds(x0, X)
-        for k in range(1, nx):
-            send(feats.at[t, own], feats.at[t, own], gx_sem, (t, k - 1), wid(z, plus(x, k, nx), c))
+        for kz in range(NZ):
+            own = ds(x0 + minus(z, kz, NZ) * Z, Z)
+            if kz:
+                arrive(feats.at[t, own], gz_sem, (t, kz - 1))
+            for k in range(1, nx):
+                send(feats.at[t, own], feats.at[t, own], gx_sem, (t, k - 1, kz), wid(z, plus(x, k, nx), c))
 
     def ag_c(t):
         for k in range(1, nx):
-            arrive(feats.at[t, ds(c0 + minus(x, k, nx) * X, X)], gx_sem, (t, k - 1))
+            for kz in range(NZ):
+                at = c0 + minus(x, k, nx) * X + minus(z, kz, NZ) * Z
+                arrive(feats.at[t, ds(at, Z)], gx_sem, (t, k - 1, kz))
         own = ds(c0, H)
         send(feats.at[t, own], feats.at[t, own], gc_sem, (t,), sibling)
 
@@ -394,7 +397,7 @@
             dma((2, T, nx1)),
             dma((2, T, NZ - 1)),
             dma((2, T, NZ - 1)),
-            dma((2, T, nx1)),
+            dma((2, T, nx1, NZ)),
             dma((2, T)),
             dma((2, ns1)),
             dma((2, 2, nx, NZ)),

time: 161 us -> 159 us (0.988)
  Pallas kernels: 155 us -> 153 us
    pallas_call x1, Pallas kernels: 155 us -> 153 us  [on_device(): pl.pallas_call(functools.partial(kernel, n, n_src), out_shape=(jax.ShapeD...]
where the time goes in v3:
time: 159 us; the launch traced here: 158 us
  Pallas kernels  153 us (96%)
  local copies, waits for them, and re-layouts  4.8 us (3%)
    pallas_call x1, Pallas kernels, on_device(): pl.pallas_call(functools.partial(kernel, n, n_src), out_shape=(jax.ShapeD...  153 us
    unnamed x2, local copies, waits for them, and re-layouts  3.24 us

profile of v3, /device:TPU:19, one launch (start us, length us, event | category | flops | bytes accessed | tf_op | source)
XLA Modules:
  0.0 158.5 jit_solution(6672936416109168459)
XLA Ops:
  0.6 0.8 dynamic_slice.3
  1.4 0.8 copy.12.ids_col
  2.2 153.0 %shard_map.113 = (bf16[256,512]{1,0:T(8,128)(2,1)}, bf16[256,256]{1,0:T(8,128)(2,1)}) custom-call(bf16[1,512,512]{2,1,0:T(8,128)(2,1)} %resid.1, bf16[1,512,6144]{2,1,0:T(8,128)(2,1)} %enc_w.1, f32[1,6144]{1,0:T(1,128)} %enc_b.1, bf16[1,6144,512]{2,1,0:T(8,128)(2,1)} %dec_w.1, bf16[512,512]{1,0:T(8,128)(2,1)} %target.1, f32[1,512]{1,0:T(1,128)} %bitcast.5, ...), custom_call_target="tpu_custom_call" | custom-call | tf_op jit(solution)/shard_map/pallas_call | solution.py:362
  155.2 1.7 %copy.15 = bf16[256,512]{1,0:T(8,128)(2,1)} copy(bf16[256,512]{1,0:T(8,128)(2,1)} %get-tuple-element.4) | data formatting | bytes 524288
  156.9 1.6 copy.16
